TPU v7x, 512 devices: a whole 4x4x16 slice. The times are simulated.
512 devices in a mesh: leaf: 32 (over x, y, core), front: 16 (over z).
Axes of the slice: x: 4, y: 4, z: 16, core: 2. Of those that a mesh axis runs over, the one named last changes fastest.
Arguments:
- panel_0: float32 [2, 1024, 1024], P(None, 'front', 'leaf'), as said below
- panel_1: float32 [2, 1024, 2048], P(None, 'front', 'leaf'), as said below
- panel_2: float32 [2, 1024, 4096], P(None, 'front', 'leaf'), as said below
- panel_3: float32 [2, 1024, 8192], P(None, 'front', 'leaf'), as said below
- load_0: float32 [1024, 128], P('leaf'), may hold values from -6 to 6
- load_1: float32 [2048, 128], P('leaf'), may hold values from -6 to 6
- load_2: float32 [4096, 128], P('leaf'), may hold values from -6 to 6
- load_3: float32 [8192, 128], P('leaf'), may hold values from -6 to 6
- inflow: float32 [8, 1024, 128], P(None, 'front'), may hold values from -6 to 6
- above_solution: float32 [1024, 128], replicated, may hold values from -6 to 6
- block_maps: int32 [14, 16], replicated, may hold values from 0 to 31, as said below
Outputs:
- solution_0: float32 [1024, 128], P(('leaf', 'front'))
- solution_1: float32 [2048, 128], P(('leaf', 'front'))
- solution_2: float32 [4096, 128], P(('leaf', 'front'))
- solution_3: float32 [8192, 128], P(('leaf', 'front'))
- top_update: float32 [1024, 128], P('front')
Inputs may be any that keep to these rules, and one draw needn't show every extreme that they name: `block_maps`: the 16 entries of each row are distinct. `panel_0`: within each front the pivot block K is lower triangular with diagonal entries of 0.8 to 1.25. `panel_1`: within each front the pivot block K is lower triangular with diagonal entries of 0.8 to 1.25. `panel_2`: within each front the pivot block K is lower triangular with diagonal entries of 0.8 to 1.25. `panel_3`: within each front the pivot block K is lower triangular with diagonal entries of 0.8 to 1.25.
All inputs are finite; a program needn't handle non-finite values.
Results may differ from a plain program's by a relative error of at most 0.00013.
Values sent between devices are 32-bit elements; how exact they have to be, the bound alone decides.
No kernel may reach another device: no remote copies, remote signals or barrier semaphores. Data moves between devices by JAX's collectives and lax.ppermute only.
A program may use at most 64 MiB of HBM per device.

v0:
```python
import jax
import jax.numpy as jnp
from jax import lax
from jax.sharding import PartitionSpec as P

exact_precision = lax.Precision.HIGHEST


def partner_2(value, axis, distance):
    mask = 2**distance
    pairs = [(source, source ^ mask) for source in range(lax.axis_size(axis))]
    return lax.ppermute(value, axis, pairs)


def group_total(partial_sum, group_bits, level_id):
    leaf_pos = lax.axis_index("leaf")
    group_count = 1 << level_id
    slot_id = leaf_pos >> group_bits
    chosen = (jnp.arange(group_count, dtype=jnp.int32) == slot_id).astype(jnp.float32)
    spread_out = chosen.reshape((group_count,) + (1,) * partial_sum.ndim) * partial_sum[None]
    totals = lax.psum(spread_out, "leaf")
    return lax.dynamic_index_in_dim(totals, slot_id, 0, keepdims=False)


def group_concat(column_block, group_bits):
    leaf_pos = lax.axis_index("leaf")
    for section_bit in range(group_bits):
        partner = partner_2(column_block, "leaf", section_bit)
        upper_half = leaf_pos >> section_bit & 1 == 1
        column_block = jnp.where(
            upper_half,
            jnp.concatenate([partner, column_block], 0),
            jnp.concatenate([column_block, partner], 0),
        )
    return column_block


def place_blocks(map_row, values, block_rows):
    block_count = map_row.shape[0]
    targets = jnp.arange(2 * block_count, dtype=jnp.int32)
    selector_matrix = (targets[:, None] == map_row[None, :]).astype(jnp.float32)
    factor_blocks = values.reshape(block_count, block_rows, values.shape[1])
    return jnp.einsum("du,uye->dye", selector_matrix, factor_blocks, precision=exact_precision)


def lift_update(update_block, level_id, group_bits, block_maps, sep_rows):
    leaf_pos = lax.axis_index("leaf")
    front_pos = lax.axis_index("front")
    block_rows = update_block.shape[0]
    block_count = sep_rows // block_rows
    group_size = 1 << group_bits
    child_id = leaf_pos >> group_bits
    base_row = (1 << level_id) - 2
    own_map = lax.dynamic_index_in_dim(block_maps, base_row + child_id, 0, keepdims=False)
    parent_pos = leaf_pos % (2 * group_size)
    parent_rows = sep_rows // (2 * group_size)
    other_map = lax.dynamic_index_in_dim(block_maps, base_row + (child_id ^ 1), 0, keepdims=False)
    partner_block = partner_2(update_block, "leaf", group_bits)
    own_full, other_full = (
        lax.all_gather(update_block, "front", axis=0, tiled=True),
        lax.all_gather(partner_block, "front", axis=0, tiled=True),
    )
    placed = place_blocks(own_map, own_full, block_rows) + place_blocks(
        other_map, other_full, block_rows
    )
    separator = placed[:block_count].reshape(sep_rows, -1)
    sep_part = lax.dynamic_slice_in_dim(separator, parent_pos * parent_rows, parent_rows, 0)
    border = lax.dynamic_index_in_dim(placed, block_count + front_pos, 0, keepdims=False)
    return (sep_part, border)


def on_device(
    panel_0,
    panel_1,
    panel_2,
    panel_3,
    load_0,
    load_1,
    load_2,
    load_3,
    inflow,
    above_solution,
    block_maps,
):
    panels = (panel_0, panel_1, panel_2, panel_3)
    load_list = (load_0, load_1, load_2, load_3)
    level_count = len(panels)
    leaf_pos = lax.axis_index("leaf")
    front_pos = lax.axis_index("front")
    front_count = lax.axis_size("front")
    total_bits = lax.axis_size("leaf").bit_length() - 1
    block_rows = panel_0.shape[1]
    sep_rows = block_rows * front_count
    solved = [None] * level_count
    lifted = None
    top_block = None
    for level_id in range(level_count - 1, -1, -1):
        group_bits = total_bits - level_id
        right_side = load_list[level_id]
        if level_id == level_count - 1:
            front_id = leaf_pos >> group_bits
            border = lax.dynamic_index_in_dim(inflow, front_id, 0, keepdims=False)
        else:
            right_side = right_side + lifted[0]
            border = lifted[1]
        partial_sum = jnp.einsum(
            "ksc,cr->ksr", panels[level_id], right_side, precision=exact_precision
        )
        totals = group_total(partial_sum, group_bits, level_id)
        solved[level_id] = totals[0]
        update_block = border - totals[1]
        if level_id > 0:
            lifted = lift_update(update_block, level_id, group_bits, block_maps, sep_rows)
        else:
            top_block = update_block
    upper_full = above_solution
    upper_block = lax.dynamic_slice_in_dim(above_solution, front_pos * block_rows, block_rows, 0)
    targets = jnp.arange(2 * front_count, dtype=jnp.int32)
    pieces = []
    for level_id in range(level_count):
        group_bits = total_bits - level_id
        stacked = jnp.stack([solved[level_id], -upper_block])
        partial_sum = jnp.einsum(
            "ksc,ksr->cr", panels[level_id], stacked, precision=exact_precision
        )
        column_block = lax.psum(partial_sum, "front")
        span_rows = column_block.shape[0] // front_count
        pieces.append(lax.dynamic_slice_in_dim(column_block, front_pos * span_rows, span_rows, 0))
        if level_id < level_count - 1:
            full_solution = group_concat(column_block, group_bits)
            ancestor_blocks = jnp.concatenate([full_solution, upper_full], 0).reshape(
                2 * front_count, block_rows, -1
            )
            child_id = leaf_pos >> group_bits - 1
            child_map = lax.dynamic_index_in_dim(
                block_maps, (2 << level_id) - 2 + child_id, 0, keepdims=False
            )
            selector_matrix = (child_map[:, None] == targets[None, :]).astype(jnp.float32)
            upper_factor_blocks = jnp.einsum(
                "gq,qzk->gzk", selector_matrix, ancestor_blocks, precision=exact_precision
            )
            upper_full = upper_factor_blocks.reshape(sep_rows, -1)
            upper_block = lax.dynamic_index_in_dim(
                upper_factor_blocks, front_pos, 0, keepdims=False
            )
    return (pieces[0], pieces[1], pieces[2], pieces[3], top_block)


def solution(mesh):
    in_specs = (
        P(None, "front", "leaf"),
        P(None, "front", "leaf"),
        P(None, "front", "leaf"),
        P(None, "front", "leaf"),
        P("leaf", None),
        P("leaf", None),
        P("leaf", None),
        P("leaf", None),
        P(None, "front", None),
        P(),
        P(),
    )
    out_specs = (
        P(("leaf", "front"), None),
        P(("leaf", "front"), None),
        P(("leaf", "front"), None),
        P(("leaf", "front"), None),
        P("front", None),
    )
    return jax.shard_map(
        on_device, mesh=mesh, in_specs=in_specs, out_specs=out_specs, check_vma=False
    )
```

profile of v0, /device:TPU:2, one launch (start us, length us, event | category | flops | bytes accessed | tf_op | source)
XLA Modules:
  0.0 1208.8 jit_solution(1407500976551751530)
XLA Ops:
  8.1 1.2 fusion.16
  11.1 138.3 %all-reduce.7.cloned.1.call-done = f32[8,2,64,128]{3,2,1,0:T(8,128)} async-done(((f32[8,2,64,128]{3,2,1,0:T(8,128)}), f32[8,2,64,128]{3,2,1,0:T(8,128)}) %all-reduce.7.cloned.1.call-update) | async-done | bytes 524304 | tf_op jit(solution)/shard_map/psum | solution.py:21
  150.2 4.2 collective-permute-start
  154.4 33.1 %all_gather.18 = f32[1024,128]{1,0:T(8,128)S(1)} all-gather(f32[64,128]{1,0:T(8,128)S(1)} %fusion.32), channel_id=1, replica_groups=mesh['leaf'=32,'front'=16] {'front'}, dimensions={0}, use_global_device_ids=true | all-gather | bytes 557056 | tf_op jit(solution)/shard_map/all_gather | solution.py:60
  188.5 30.6 %all_gather.19 = f32[1024,128]{1,0:T(8,128)S(1)} all-gather(f32[64,128]{1,0:T(8,128)S(1)} %collective-permute-done), channel_id=1, replica_groups=mesh['leaf'=32,'front'=16] {'front'}, dimensions={0}, use_global_device_ids=true | all-gather | bytes 557056 | tf_op jit(solution)/shard_map/all_gather | solution.py:61
  219.1 1.0 convolution_add_fusion.2
  222.2 127.9 %all-reduce.9.cloned.1.call-done = f32[4,2,64,128]{3,2,1,0:T(8,128)} async-done(((f32[4,2,64,128]{3,2,1,0:T(8,128)}), f32[4,2,64,128]{3,2,1,0:T(8,128)}) %all-reduce.9.cloned.1.call-update) | async-done | bytes 262160 | tf_op jit(solution)/shard_map/psum | solution.py:21
  350.8 3.0 collective-permute-start.1
  353.8 33.6 %all_gather.20 = f32[1024,128]{1,0:T(8,128)S(1)} all-gather(f32[64,128]{1,0:T(8,128)S(1)} %fusion.31), channel_id=1, replica_groups=mesh['leaf'=32,'front'=16] {'front'}, dimensions={0}, use_global_device_ids=true | all-gather | bytes 557056 | tf_op jit(solution)/shard_map/all_gather | solution.py:60
  388.3 30.1 %all_gather.21 = f32[1024,128]{1,0:T(8,128)S(1)} all-gather(f32[64,128]{1,0:T(8,128)S(1)} %collective-permute-done.1), channel_id=1, replica_groups=mesh['leaf'=32,'front'=16] {'front'}, dimensions={0}, use_global_device_ids=true | all-gather | bytes 557056 | tf_op jit(solution)/shard_map/all_gather | solution.py:61
  421.3 126.1 %all-reduce.11.cloned.1.call-done = f32[2,2,64,128]{3,2,1,0:T(8,128)} async-done(((f32[2,2,64,128]{3,2,1,0:T(8,128)}), f32[2,2,64,128]{3,2,1,0:T(8,128)}) %all-reduce.11.cloned.1.call-update) | async-done | bytes 131088 | tf_op jit(solution)/shard_map/psum | solution.py:21
  548.2 5.2 collective-permute-start.2
  553.4 33.3 %all_gather.22 = f32[1024,128]{1,0:T(8,128)S(1)} all-gather(f32[64,128]{1,0:T(8,128)S(1)} %fusion.30), channel_id=1, replica_groups=mesh['leaf'=32,'front'=16] {'front'}, dimensions={0}, use_global_device_ids=true | all-gather | bytes 557056 | tf_op jit(solution)/shard_map/all_gather | solution.py:60
  587.6 30.3 %all_gather.23 = f32[1024,128]{1,0:T(8,128)S(1)} all-gather(f32[64,128]{1,0:T(8,128)S(1)} %collective-permute-done.2), channel_id=1, replica_groups=mesh['leaf'=32,'front'=16] {'front'}, dimensions={0}, use_global_device_ids=true | all-gather | bytes 557056 | tf_op jit(solution)/shard_map/all_gather | solution.py:61
  617.9 1.0 convolution_add_fusion
  620.7 120.9 %all-reduce.13.cloned.1.call-done = f32[1,2,64,128]{3,2,1,0:T(8,128)} async-done(((f32[1,2,64,128]{3,2,1,0:T(8,128)}), f32[1,2,64,128]{3,2,1,0:T(8,128)}) %all-reduce.13.cloned.1.call-update) | async-done | bytes 65552 | tf_op jit(solution)/shard_map/psum | solution.py:21
  742.6 56.8 %psum.60 = f32[32,128]{1,0:T(8,128)S(1)} all-reduce(f32[32,128]{1,0:T(8,128)S(1)} %convolution_bitcast_fusion.5), channel_id=1, replica_groups=mesh['leaf'=32,'front'=16] {'front'}, use_global_device_ids=true, to_apply=%region_4.5 | all-reduce | flops 4096 | bytes 32768 | tf_op jit(solution)/shard_map/psum | solution.py:126
  799.4 1.9 collective-permute-start.3
  801.3 1.1 collective-permute-done.3
  802.4 3.4 collective-permute-start.4
  805.8 2.4 collective-permute-done.4
  808.2 4.6 collective-permute-start.5
  812.8 3.1 collective-permute-done.5
  815.9 3.3 collective-permute-start.6
  819.3 3.5 collective-permute-done.6
  822.8 4.1 collective-permute-start.7
  827.6 4.9 collective-permute-done.7
  832.7 1.1 fusion.5
  834.2 53.5 %psum.61 = f32[64,128]{1,0:T(8,128)S(1)} all-reduce(f32[64,128]{1,0:T(8,128)S(1)} %convolution_bitcast_fusion.4), channel_id=1, replica_groups=mesh['leaf'=32,'front'=16] {'front'}, use_global_device_ids=true, to_apply=%region_5.6 | all-reduce | flops 8192 | bytes 65536 | tf_op jit(solution)/shard_map/psum | solution.py:126
  887.7 1.9 collective-permute-start.8
  889.6 1.2 collective-permute-done.8
  890.8 3.4 collective-permute-start.9
  894.1 2.8 collective-permute-done.9
  896.9 4.6 collective-permute-start.10
  901.5 3.8 collective-permute-done.10
  905.3 3.5 collective-permute-start.11
  909.8 3.8 collective-permute-done.11
  913.7 1.1 fusion.3
  915.9 129.0 %all-reduce.15.cloned.1.call-done = f32[128,128]{0,1:T(8,128)} async-done(((f32[128,128]{0,1:T(8,128)}), f32[128,128]{0,1:T(8,128)}) %all-reduce.15.cloned.1.call-update) | async-done | bytes 65552 | tf_op jit(solution)/shard_map/psum | solution.py:126
  1044.9 1.9 collective-permute-start.12
  1046.8 1.4 collective-permute-done.12
  1049.1 3.4 collective-permute-start.13
  1053.4 3.2 collective-permute-done.13
  1056.6 4.9 collective-permute-start.14
  1063.1 4.4 collective-permute-done.14
  1068.0 1.1 fusion.1
  1069.2 1.0 convolution_bitcast_fusion
  1071.7 128.7 %all-reduce.17.cloned.1.call-done = f32[256,128]{0,1:T(8,128)} async-done(((f32[256,128]{0,1:T(8,128)}), f32[256,128]{0,1:T(8,128)}) %all-reduce.17.cloned.1.call-update) | async-done | bytes 131088 | tf_op jit(solution)/shard_map/psum | solution.py:126
  (101 shorter events, 25.7 us)
Async XLA Ops:
  7.2 0.9 copy-start
  7.2 142.3 %all-reduce.7.cloned.1.call-start = ((), (), s32[]{:S(2)}) async-start(), calls=%async_computation | async-start | bytes 1048576 | tf_op jit(solution)/shard_map/psum | solution.py:21
  10.2 339.9 %all-reduce.9.cloned.1.call-start = ((), (), s32[]{:S(2)}) async-start(), calls=%async_computation.1 | async-start | bytes 524288 | tf_op jit(solution)/shard_map/psum | solution.py:21
  150.2 38.2 %collective-permute-start = (f32[64,128]{1,0:T(8,128)S(1)}, f32[64,128]{1,0:T(8,128)S(1)}, u32[]{:S(2)}, u32[]{:S(2)}) collective-permute-start(f32[64,128]{1,0:T(8,128)S(1)} %fusion.32), channel_id=1, source_target_pairs={{0,64},{16,80},{32,96},{48,112},{64,0},{80,16},{96,32},{112,48},{1... | collective-permute-start | bytes 98312 | tf_op jit(solution)/shard_map/ppermute | solution.py:12
  220.1 0.8 copy-start.3
  220.1 0.9 copy-start.7
  222.0 325.4 %all-reduce.11.cloned.1.call-start = ((), (), s32[]{:S(2)}) async-start(), calls=%async_computation.2 | async-start | bytes 262144 | tf_op jit(solution)/shard_map/psum | solution.py:21
  350.8 37.5 %collective-permute-start.1 = (f32[64,128]{1,0:T(8,128)S(1)}, f32[64,128]{1,0:T(8,128)S(1)}, u32[]{:S(2)}, u32[]{:S(2)}) collective-permute-start(f32[64,128]{1,0:T(8,128)S(1)} %fusion.31), channel_id=1, source_target_pairs={{0,128},{16,144},{32,160},{48,176},{64,192},{80,208},{96,224},{112... | collective-permute-start | bytes 98312 | tf_op jit(solution)/shard_map/ppermute | solution.py:12
  419.4 0.8 copy-start.2
  419.5 0.8 copy-start.8
  421.2 320.4 %all-reduce.13.cloned.1.call-start = ((), (), s32[]{:S(2)}) async-start(), calls=%async_computation.3 | async-start | bytes 131072 | tf_op jit(solution)/shard_map/psum | solution.py:21
  548.2 39.5 %collective-permute-start.2 = (f32[64,128]{1,0:T(8,128)S(1)}, f32[64,128]{1,0:T(8,128)S(1)}, u32[]{:S(2)}, u32[]{:S(2)}) collective-permute-start(f32[64,128]{1,0:T(8,128)S(1)} %fusion.30), channel_id=1, source_target_pairs={{0,256},{16,272},{32,288},{48,304},{64,320},{80,336},{96,352},{112... | collective-permute-start | bytes 98312 | tf_op jit(solution)/shard_map/ppermute | solution.py:12
  618.9 0.8 copy-start.5
  619.0 0.8 copy-start.9
  619.0 1.7 copy-start.1
  620.7 424.2 %all-reduce.15.cloned.1.call-start = ((), (), s32[]{:S(2)}) async-start(), calls=%async_computation.4 | async-start | bytes 131072 | tf_op jit(solution)/shard_map/psum | solution.py:126
  799.4 3.1 collective-permute-start.3
  802.4 5.8 collective-permute-start.4
  808.2 7.7 collective-permute-start.5
  815.9 6.9 collective-permute-start.6
  822.8 9.8 collective-permute-start.7
  887.7 3.1 collective-permute-start.8
  890.8 6.2 collective-permute-start.9
  896.9 8.4 collective-permute-start.10
  905.3 8.3 collective-permute-start.11
  915.9 284.5 %all-reduce.17.cloned.1.call-start = ((), (), s32[]{:S(2)}) async-start(), calls=%async_computation.5 | async-start | bytes 262144 | tf_op jit(solution)/shard_map/psum | solution.py:126
  1044.9 3.3 collective-permute-start.12
  1049.1 7.5 collective-permute-start.13
  1053.4 8.8 copy-start.6
  1056.6 10.9 collective-permute-start.14
  1070.1 0.8 copy-start.4
Sparse Core Ops, SparseCore 0:
  11.2 138.1 all-reduce.6
  222.1 127.8 all-reduce.8
  421.4 126.0 all-reduce.10
  620.8 120.7 all-reduce.12
  916.0 128.8 all-reduce.14
  1070.3 130.0 all-reduce.16
where the time goes:
time: 1210 us
  waiting for transfers between devices  806 us (67%)
  blocking collectives  301 us (25%)
  starting transfers between devices  53.6 us (4%)
  between operations  14.8 us (1%)
  matrix products  13.7 us (1%)
    psum x4, waiting for transfers between devices, group_total(): totals = lax.psum(spread_out, 'leaf')  513 us
    psum x2, waiting for transfers between devices, on_device(): column_block = lax.psum(partial_sum, 'front')  258 us
    psum x2, blocking collectives, on_device(): column_block = lax.psum(partial_sum, 'front')  110 us
    all_gather x3, blocking collectives, lift_update(): lax.all_gather(update_block, 'front', axis=0, tiled=True)  100 us
    all_gather x3, blocking collectives, lift_update(): lax.all_gather(partner_block, 'front', axis=0, tiled=True)  91 us
    ppermute x15, starting transfers between devices, partner_2(): return lax.ppermute(value, axis, pairs)  53.4 us
    ppermute x15, waiting for transfers between devices, partner_2(): return lax.ppermute(value, axis, pairs)  35.6 us
  transfers between devices with their start and end apart: 21, of which 18 were waited for; matrix products, arithmetic and copies ran while one was open for 1% of the time, Pallas kernels for 0%

commit v1 on v0

--- a/solution.py
+++ b/solution.py
@@ -4,6 +4,14 @@
 from jax.sharding import PartitionSpec as P
 
 exact_precision = lax.Precision.HIGHEST
+
+
+def add_in_pairs(x, name):
+    devices, acc = (lax.axis_size(name), x)
+    for stride in [1 << k for k in range(devices.bit_length() - 1)]:
+        route = [(i, i ^ stride) for i in range(devices)]
+        acc = acc + lax.ppermute(acc, name, route)
+    return acc
 
 
 def partner_2(value, axis, distance):
@@ -18,7 +26,7 @@
     slot_id = leaf_pos >> group_bits
     chosen = (jnp.arange(group_count, dtype=jnp.int32) == slot_id).astype(jnp.float32)
     spread_out = chosen.reshape((group_count,) + (1,) * partial_sum.ndim) * partial_sum[None]
-    totals = lax.psum(spread_out, "leaf")
+    totals = add_in_pairs(spread_out, "leaf")
     return lax.dynamic_index_in_dim(totals, slot_id, 0, keepdims=False)
 
 

time: 1210 us -> 856 us (0.71)
  waiting for transfers between devices: 806 us -> 408 us
  starting transfers between devices: 53.6 us -> 112 us
    psum x4 -> x0, waiting for transfers between devices: 513 us -> none  [group_total(): totals = lax.psum(spread_out, 'leaf')]
    ppermute x0 -> x20, waiting for transfers between devices: none -> 111 us  [add_in_pairs(): acc = acc + lax.ppermute(acc, name, route)]
    ppermute x0 -> x20, starting transfers between devices: none -> 65 us  [add_in_pairs(): acc = acc + lax.ppermute(acc, name, route)]
  transfers between devices with their start and end apart: 21 -> 37, of which waited for: 18 -> 34; matrix products, arithmetic and copies ran while one was open for 1% -> 1% of each run, Pallas kernels for 0% -> 0%
where the time goes in v1:
time: 856 us; the launch traced here: 855 us
  waiting for transfers between devices  408 us (48%)
  blocking collectives  293 us (34%)
  starting transfers between devices  112 us (13%)
  between operations  15.1 us (2%)
  matrix products  13.1 us (2%)
  local copies, waits for them, and re-layouts  10.4 us (1%)
    psum x2, waiting for transfers between devices, on_device(): column_block = lax.psum(partial_sum, 'front')  255 us
    ppermute x20, waiting for transfers between devices, add_in_pairs(): acc = acc + lax.ppermute(acc, name, route)  111 us
    psum x2, blocking collectives, on_device(): column_block = lax.psum(partial_sum, 'front')  107 us
    all_gather x3, blocking collectives, lift_update(): lax.all_gather(update_block, 'front', axis=0, tiled=True)  99 us
    all_gather x3, blocking collectives, lift_update(): lax.all_gather(partner_block, 'front', axis=0, tiled=True)  86.3 us
    ppermute x20, starting transfers between devices, add_in_pairs(): acc = acc + lax.ppermute(acc, name, route)  65 us
    ppermute x15, starting transfers between devices, partner_2(): return lax.ppermute(value, axis, pairs)  46.7 us
    ppermute x15, waiting for transfers between devices, partner_2(): return lax.ppermute(value, axis, pairs)  41.7 us
  transfers between devices with their start and end apart: 37, of which 34 were waited for; matrix products, arithmetic and copies ran while one was open for 1% of the time, Pallas kernels for 0%

profile of v1, /device:TPU:2, one launch (start us, length us, event | category | flops | bytes accessed | tf_op | source)
XLA Modules:
  0.0 854.6 jit_solution(5856727346833359832)
XLA Ops:
  13.3 3.5 collective-permute-start.1
  16.8 12.4 %collective-permute-done.1 = f32[8,2,64,128]{3,2,1,0:T(8,128)S(1)} collective-permute-done((f32[8,2,64,128]{3,2,1,0:T(8,128)S(1)}, f32[8,2,64,128]{3,2,1,0:T(8,128)S(1)}, u32[]{:S(2)}, u32[]{:S(2)}) %collective-permute-start.1) | collective-permute-done | bytes 524320 | tf_op jit(solution)/shard_map/ppermute | solution.py:13
  29.3 5.1 collective-permute-start.2
  34.4 11.4 %collective-permute-done.2 = f32[8,2,64,128]{3,2,1,0:T(8,128)S(1)} collective-permute-done((f32[8,2,64,128]{3,2,1,0:T(8,128)S(1)}, f32[8,2,64,128]{3,2,1,0:T(8,128)S(1)}, u32[]{:S(2)}, u32[]{:S(2)}) %collective-permute-start.2) | collective-permute-done | bytes 524320 | tf_op jit(solution)/shard_map/ppermute | solution.py:13
  45.9 7.8 collective-permute-start.3
  53.7 10.5 %collective-permute-done.3 = f32[8,2,64,128]{3,2,1,0:T(8,128)S(1)} collective-permute-done((f32[8,2,64,128]{3,2,1,0:T(8,128)S(1)}, f32[8,2,64,128]{3,2,1,0:T(8,128)S(1)}, u32[]{:S(2)}, u32[]{:S(2)}) %collective-permute-start.3) | collective-permute-done | bytes 524320 | tf_op jit(solution)/shard_map/ppermute | solution.py:13
  67.1 12.1 %collective-permute-done.4 = f32[8,2,64,128]{3,2,1,0:T(8,128)S(1)} collective-permute-done((f32[8,2,64,128]{3,2,1,0:T(8,128)S(1)}, f32[8,2,64,128]{3,2,1,0:T(8,128)S(1)}, u32[]{:S(2)}, u32[]{:S(2)}) %collective-permute-start.4) | collective-permute-done | bytes 524320 | tf_op jit(solution)/shard_map/ppermute | solution.py:13
  82.8 36.3 %all_gather.18 = f32[1024,128]{1,0:T(8,128)S(1)} all-gather(f32[64,128]{1,0:T(8,128)S(1)} %fusion.34), channel_id=1, replica_groups=mesh['leaf'=32,'front'=16] {'front'}, dimensions={0}, use_global_device_ids=true | all-gather | bytes 557056 | tf_op jit(solution)/shard_map/all_gather | solution.py:68
  120.0 28.7 %all_gather.19 = f32[1024,128]{1,0:T(8,128)S(1)} all-gather(f32[64,128]{1,0:T(8,128)S(1)} %collective-permute-done.5), channel_id=1, replica_groups=mesh['leaf'=32,'front'=16] {'front'}, dimensions={0}, use_global_device_ids=true | all-gather | bytes 557056 | tf_op jit(solution)/shard_map/all_gather | solution.py:69
  156.9 7.8 collective-permute-done.7
  167.5 8.2 collective-permute-done.8
  178.2 6.0 collective-permute-done.9
  184.2 4.0 collective-permute-start.10
  188.4 5.6 collective-permute-done.10
  196.5 31.4 %all_gather.20 = f32[1024,128]{1,0:T(8,128)S(1)} all-gather(f32[64,128]{1,0:T(8,128)S(1)} %fusion.33), channel_id=1, replica_groups=mesh['leaf'=32,'front'=16] {'front'}, dimensions={0}, use_global_device_ids=true | all-gather | bytes 557056 | tf_op jit(solution)/shard_map/all_gather | solution.py:68
  228.8 28.7 %all_gather.21 = f32[1024,128]{1,0:T(8,128)S(1)} all-gather(f32[64,128]{1,0:T(8,128)S(1)} %collective-permute-done.11), channel_id=1, replica_groups=mesh['leaf'=32,'front'=16] {'front'}, dimensions={0}, use_global_device_ids=true | all-gather | bytes 557056 | tf_op jit(solution)/shard_map/all_gather | solution.py:69
  265.8 4.7 collective-permute-done.13
  270.6 3.9 collective-permute-start.14
  274.5 4.5 collective-permute-done.14
  279.0 3.4 collective-permute-start.15
  282.4 3.5 collective-permute-done.15
  285.8 4.3 collective-permute-start.16
  290.3 3.9 collective-permute-done.16
  294.2 4.3 collective-permute-start.17
  298.6 31.4 %all_gather.22 = f32[1024,128]{1,0:T(8,128)S(1)} all-gather(f32[64,128]{1,0:T(8,128)S(1)} %fusion.32), channel_id=1, replica_groups=mesh['leaf'=32,'front'=16] {'front'}, dimensions={0}, use_global_device_ids=true | all-gather | bytes 557056 | tf_op jit(solution)/shard_map/all_gather | solution.py:68
  330.9 28.9 %all_gather.23 = f32[1024,128]{1,0:T(8,128)S(1)} all-gather(f32[64,128]{1,0:T(8,128)S(1)} %collective-permute-done.17), channel_id=1, replica_groups=mesh['leaf'=32,'front'=16] {'front'}, dimensions={0}, use_global_device_ids=true | all-gather | bytes 557056 | tf_op jit(solution)/shard_map/all_gather | solution.py:69
  367.4 3.7 collective-permute-done.19
  371.2 3.9 collective-permute-start.20
  375.0 3.8 collective-permute-done.20
  378.8 3.7 collective-permute-start.21
  388.0 4.6 collective-permute-done.22
  392.9 54.6 %psum.28 = f32[32,128]{1,0:T(8,128)S(1)} all-reduce(f32[32,128]{1,0:T(8,128)S(1)} %convolution_bitcast_fusion.5), channel_id=1, replica_groups=mesh['leaf'=32,'front'=16] {'front'}, use_global_device_ids=true, to_apply=%region_0.1 | all-reduce | flops 4096 | bytes 32768 | tf_op jit(solution)/shard_map/psum | solution.py:134
  456.4 3.6 collective-permute-start.25
  460.0 4.0 collective-permute-done.25
  464.0 3.9 collective-permute-start.26
  474.0 6.7 collective-permute-done.27
  483.0 52.7 %psum.29 = f32[64,128]{1,0:T(8,128)S(1)} all-reduce(f32[64,128]{1,0:T(8,128)S(1)} %convolution_bitcast_fusion.4), channel_id=1, replica_groups=mesh['leaf'=32,'front'=16] {'front'}, use_global_device_ids=true, to_apply=%region_1.2 | all-reduce | flops 8192 | bytes 65536 | tf_op jit(solution)/shard_map/psum | solution.py:134
  541.3 3.7 collective-permute-done.29
  544.9 3.6 collective-permute-start.30
  548.6 4.7 collective-permute-done.30
  553.3 3.9 collective-permute-start.31
  557.5 4.1 collective-permute-done.31
  564.6 126.0 %all-reduce.3.cloned.1.call-done = f32[128,128]{0,1:T(8,128)} async-done(((f32[128,128]{0,1:T(8,128)}), f32[128,128]{0,1:T(8,128)}) %all-reduce.3.cloned.1.call-update) | async-done | bytes 65552 | tf_op jit(solution)/shard_map/psum | solution.py:134
  694.9 3.4 collective-permute-start.33
  698.4 4.0 collective-permute-done.33
  702.4 4.9 collective-permute-start.34
  708.9 4.4 collective-permute-done.34
  717.5 128.7 %all-reduce.5.cloned.1.call-done = f32[256,128]{0,1:T(8,128)} async-done(((f32[256,128]{0,1:T(8,128)}), f32[256,128]{0,1:T(8,128)}) %all-reduce.5.cloned.1.call-update) | async-done | bytes 131088 | tf_op jit(solution)/shard_map/psum | solution.py:134
  (153 shorter events, 90.5 us)
Async XLA Ops:
  7.2 0.9 copy-start
  7.2 683.5 %all-reduce.3.cloned.1.call-start = ((), (), s32[]{:S(2)}) async-start(), calls=%async_computation | async-start | bytes 131072 | tf_op jit(solution)/shard_map/psum | solution.py:134
  9.4 3.8 collective-permute-start
  13.3 15.9 %collective-permute-start.1 = (f32[8,2,64,128]{3,2,1,0:T(8,128)S(1)}, f32[8,2,64,128]{3,2,1,0:T(8,128)S(1)}, u32[]{:S(2)}, u32[]{:S(2)}) collective-permute-start(f32[8,2,64,128]{3,2,1,0:T(8,128)S(1)} %fusion.16), channel_id=1, source_target_pairs={{0,32},{16,48},{32,0},{48,16},{64,96},{80,112},{96,64},{112,80},{1... | collective-permute-start | bytes 1572872 | tf_op jit(solution)/shard_map/ppermute | solution.py:13
  29.3 16.5 %collective-permute-start.2 = (f32[8,2,64,128]{3,2,1,0:T(8,128)S(1)}, f32[8,2,64,128]{3,2,1,0:T(8,128)S(1)}, u32[]{:S(2)}, u32[]{:S(2)}) collective-permute-start(f32[8,2,64,128]{3,2,1,0:T(8,128)S(1)} %fusion.90), channel_id=1, source_target_pairs={{0,64},{16,80},{32,96},{48,112},{64,0},{80,16},{96,32},{112,48},{1... | collective-permute-start | bytes 1572872 | tf_op jit(solution)/shard_map/ppermute | solution.py:13
  45.9 18.3 %collective-permute-start.3 = (f32[8,2,64,128]{3,2,1,0:T(8,128)S(1)}, f32[8,2,64,128]{3,2,1,0:T(8,128)S(1)}, u32[]{:S(2)}, u32[]{:S(2)}) collective-permute-start(f32[8,2,64,128]{3,2,1,0:T(8,128)S(1)} %add.205), channel_id=1, source_target_pairs={{0,128},{16,144},{32,160},{48,176},{64,192},{80,208},{96,224},{112... | collective-permute-start | bytes 1572872 | tf_op jit(solution)/shard_map/ppermute | solution.py:13
  64.2 15.0 %collective-permute-start.4 = (f32[8,2,64,128]{3,2,1,0:T(8,128)S(1)}, f32[8,2,64,128]{3,2,1,0:T(8,128)S(1)}, u32[]{:S(2)}, u32[]{:S(2)}) collective-permute-start(f32[8,2,64,128]{3,2,1,0:T(8,128)S(1)} %add.206), channel_id=1, source_target_pairs={{0,256},{16,272},{32,288},{48,304},{64,320},{80,336},{96,352},{112... | collective-permute-start | bytes 1572872 | tf_op jit(solution)/shard_map/ppermute | solution.py:13
  80.0 40.0 %collective-permute-start.5 = (f32[64,128]{1,0:T(8,128)S(1)}, f32[64,128]{1,0:T(8,128)S(1)}, u32[]{:S(2)}, u32[]{:S(2)}) collective-permute-start(f32[64,128]{1,0:T(8,128)S(1)} %fusion.34), channel_id=1, source_target_pairs={{0,64},{16,80},{32,96},{48,112},{64,0},{80,16},{96,32},{112,48},{1... | collective-permute-start | bytes 98312 | tf_op jit(solution)/shard_map/ppermute | solution.py:20
  149.7 0.8 copy-start.5
  149.7 0.9 copy-start.8
  150.9 3.4 collective-permute-start.6
  154.4 10.2 %collective-permute-start.7 = (f32[4,2,64,128]{3,2,1,0:T(8,128)S(1)}, f32[4,2,64,128]{3,2,1,0:T(8,128)S(1)}, u32[]{:S(2)}, u32[]{:S(2)}) collective-permute-start(f32[4,2,64,128]{3,2,1,0:T(8,128)S(1)} %fusion.30), channel_id=1, source_target_pairs={{0,32},{16,48},{32,0},{48,16},{64,96},{80,112},{96,64},{112,80},{1... | collective-permute-start | bytes 786440 | tf_op jit(solution)/shard_map/ppermute | solution.py:13
  164.8 10.9 %collective-permute-start.8 = (f32[4,2,64,128]{3,2,1,0:T(8,128)S(1)}, f32[4,2,64,128]{3,2,1,0:T(8,128)S(1)}, u32[]{:S(2)}, u32[]{:S(2)}) collective-permute-start(f32[4,2,64,128]{3,2,1,0:T(8,128)S(1)} %fusion.89), channel_id=1, source_target_pairs={{0,64},{16,80},{32,96},{48,112},{64,0},{80,16},{96,32},{112,48},{1... | collective-permute-start | bytes 786440 | tf_op jit(solution)/shard_map/ppermute | solution.py:13
  175.7 8.5 collective-permute-start.9
  184.2 9.8 %collective-permute-start.10 = (f32[4,2,64,128]{3,2,1,0:T(8,128)S(1)}, f32[4,2,64,128]{3,2,1,0:T(8,128)S(1)}, u32[]{:S(2)}, u32[]{:S(2)}) collective-permute-start(f32[4,2,64,128]{3,2,1,0:T(8,128)S(1)} %add.219), channel_id=1, source_target_pairs={{0,256},{16,272},{32,288},{48,304},{64,320},{80,336},{96,352},{112... | collective-permute-start | bytes 786440 | tf_op jit(solution)/shard_map/ppermute | solution.py:13
  194.0 363.2 %copy-start.2 = (f32[1,2,64,128]{3,2,1,0:T(8,128)}, f32[1,2,64,128]{3,2,1,0:T(8,128)S(1)}, u32[]{:S(2)}) copy-start(f32[1,2,64,128]{3,2,1,0:T(8,128)S(1)} %dynamic-slice_add_fusion.1) | copy-start | bytes 196612
  194.1 34.8 %collective-permute-start.11 = (f32[64,128]{1,0:T(8,128)S(1)}, f32[64,128]{1,0:T(8,128)S(1)}, u32[]{:S(2)}, u32[]{:S(2)}) collective-permute-start(f32[64,128]{1,0:T(8,128)S(1)} %fusion.33), channel_id=1, source_target_pairs={{0,128},{16,144},{32,160},{48,176},{64,192},{80,208},{96,224},{112... | collective-permute-start | bytes 98312 | tf_op jit(solution)/shard_map/ppermute | solution.py:20
  258.6 0.8 copy-start.4
  258.6 0.8 copy-start.9
  259.7 3.2 collective-permute-start.12
  263.0 7.4 collective-permute-start.13
  270.6 8.4 collective-permute-start.14
  279.0 6.9 collective-permute-start.15
  285.8 8.4 collective-permute-start.16
  294.2 179.8 %copy-start.3 = (f32[1,2,64,128]{3,2,1,0:T(8,128)}, f32[1,2,64,128]{3,2,1,0:T(8,128)S(1)}, u32[]{:S(2)}) copy-start(f32[1,2,64,128]{3,2,1,0:T(8,128)S(1)} %dynamic-slice_add_fusion) | copy-start | bytes 196612
  294.2 36.6 %collective-permute-start.17 = (f32[64,128]{1,0:T(8,128)S(1)}, f32[64,128]{1,0:T(8,128)S(1)}, u32[]{:S(2)}, u32[]{:S(2)}) collective-permute-start(f32[64,128]{1,0:T(8,128)S(1)} %fusion.32), channel_id=1, source_target_pairs={{0,256},{16,272},{32,288},{48,304},{64,320},{80,336},{96,352},{112... | collective-permute-start | bytes 98312 | tf_op jit(solution)/shard_map/ppermute | solution.py:20
  360.8 0.8 copy-start.7
  361.0 27.1 %copy-start.1 = (f32[1024,128]{1,0:T(8,128)S(1)}, f32[1024,128]{1,0:T(8,128)}, u32[]{:S(2)}) copy-start(f32[1024,128]{1,0:T(8,128)} %param.20) | copy-start | bytes 1572868
  361.8 3.1 collective-permute-start.18
  365.0 6.2 collective-permute-start.19
  371.2 7.7 collective-permute-start.20
  378.8 6.2 collective-permute-start.21
  385.0 7.7 collective-permute-start.22
  447.5 3.1 collective-permute-start.23
  450.5 5.8 collective-permute-start.24
  456.4 7.7 collective-permute-start.25
  464.0 6.9 collective-permute-start.26
  470.9 9.8 %collective-permute-start.27 = (f32[512,128]{1,0:T(8,128)S(1)}, f32[512,128]{1,0:T(8,128)S(1)}, u32[]{:S(2)}, u32[]{:S(2)}) collective-permute-start(f32[512,128]{1,0:T(8,128)S(1)} %maximum_select_fusion.3), channel_id=1, source_target_pairs={{0,256},{16,272},{32,288},{48,304},{64,320},{80,336},{96,352},{112... | collective-permute-start | bytes 786440 | tf_op jit(solution)/shard_map/ppermute | solution.py:20
  481.9 0.8 slice-start.1
  535.7 3.1 collective-permute-start.28
  538.8 6.2 collective-permute-start.29
  544.9 8.4 collective-permute-start.30
  553.3 8.3 collective-permute-start.31
  564.6 281.6 %all-reduce.5.cloned.1.call-start = ((), (), s32[]{:S(2)}) async-start(), calls=%async_computation.1 | async-start | bytes 262144 | tf_op jit(solution)/shard_map/psum | solution.py:134
  690.6 3.3 collective-permute-start.32
  694.9 7.5 collective-permute-start.33
  702.4 10.9 %collective-permute-start.34 = (f32[512,128]{0,1:T(8,128)S(1)}, f32[512,128]{0,1:T(8,128)S(1)}, u32[]{:S(2)}, u32[]{:S(2)}) collective-permute-start(f32[512,128]{0,1:T(8,128)S(1)} %maximum_select_fusion.5), channel_id=1, source_target_pairs={{0,64},{16,80},{32,96},{48,112},{64,0},{80,16},{96,32},{112,48},{1... | collective-permute-start | bytes 786440 | tf_op jit(solution)/shard_map/ppermute | solution.py:20
  715.9 0.8 copy-start.6
  (2 other events, 1.5 us)
Sparse Core Ops, SparseCore 0:
  564.7 125.8 all-reduce.2
  716.1 130.0 all-reduce.4
